TPU v7x, 128 devices: a whole 4x4x4 slice. The times are simulated.
128 devices in a mesh: dp: 4 (over y), seq: 16 (over x, z), tensor: 2 (over core).
Axes of the slice: x: 4, y: 4, z: 4, core: 2. Of those that a mesh axis runs over, the one named last changes fastest.
Arguments:
- tokens: float32 [10240, 2560], P(('dp', 'seq')), may hold values from -6 to 6
- cotangent: float32 [10240, 2560], P(('dp', 'seq')), may hold values from -6 to 6
- w_query: float32 [2560, 2560], P(('dp', 'seq'), 'tensor'), may hold values from -0.125 to 0.125
- w_keyvalue: float32 [2560, 2, 256], P(('dp', 'seq')), may hold values from -0.125 to 0.125
- w_out: float32 [2560, 2560], P('tensor', ('dp', 'seq')), may hold values from -2.5 to 2.5
- w_gateup: float32 [2560, 2, 7680], P(('dp', 'seq'), None, 'tensor'), may hold values from -0.125 to 0.125
- w_down: float32 [7680, 2560], P('tensor', ('dp', 'seq')), may hold values from -0.09375 to 0.09375
- norm_scales: float32 [2, 2560], P(None, ('dp', 'seq')), may hold values from -0.8 to 0.8
- first_query: float32 [2560, 2560], P(('dp', 'seq'), 'tensor'), may hold values from -96 to 96
- first_keyvalue: float32 [2560, 2, 256], P(('dp', 'seq')), may hold values from -192 to 192
- first_out: float32 [2560, 2560], P('tensor', ('dp', 'seq')), may hold values from -5 to 5
- first_gateup: float32 [2560, 2, 7680], P(('dp', 'seq'), None, 'tensor'), may hold values from -32 to 32
- first_down: float32 [7680, 2560], P('tensor', ('dp', 'seq')), may hold values from -40 to 40
- first_scales: float32 [2, 2560], P(None, ('dp', 'seq')), may hold values from -112 to 112
- second_query: float32 [2560, 2560], P(('dp', 'seq'), 'tensor'), may hold values from 1228.8 to 4812.8
- second_keyvalue: float32 [2560, 2, 256], P(('dp', 'seq')), may hold values from 4812.8 to 19456
- second_out: float32 [2560, 2560], P('tensor', ('dp', 'seq')), may hold values from 2.5 to 10
- second_gateup: float32 [2560, 2, 7680], P(('dp', 'seq'), None, 'tensor'), may hold values from 133.12 to 542.72
- second_down: float32 [7680, 2560], P('tensor', ('dp', 'seq')), may hold values from 225.28 to 901.12
- second_scales: float32 [2, 2560], P(None, ('dp', 'seq')), may hold values from 1331.2 to 5427.2
Outputs:
- output: float32 [10240, 2560], P(('dp', 'seq'))
- grad_tokens: float32 [10240, 2560], P(('dp', 'seq'))
- new_query: float32 [2560, 2560], P(('dp', 'seq'), 'tensor')
- new_keyvalue: float32 [2560, 2, 256], P(('dp', 'seq'))
- new_out: float32 [2560, 2560], P('tensor', ('dp', 'seq'))
- new_gateup: float32 [2560, 2, 7680], P(('dp', 'seq'), None, 'tensor')
- new_down: float32 [7680, 2560], P('tensor', ('dp', 'seq'))
- new_scales: float32 [2, 2560], P(None, ('dp', 'seq'))
- new_first_query: float32 [2560, 2560], P(('dp', 'seq'), 'tensor')
- new_first_keyvalue: float32 [2560, 2, 256], P(('dp', 'seq'))
- new_first_out: float32 [2560, 2560], P('tensor', ('dp', 'seq'))
- new_first_gateup: float32 [2560, 2, 7680], P(('dp', 'seq'), None, 'tensor')
- new_first_down: float32 [7680, 2560], P('tensor', ('dp', 'seq'))
- new_first_scales: float32 [2, 2560], P(None, ('dp', 'seq'))
- new_second_query: float32 [2560, 2560], P(('dp', 'seq'), 'tensor')
- new_second_keyvalue: float32 [2560, 2, 256], P(('dp', 'seq'))
- new_second_out: float32 [2560, 2560], P('tensor', ('dp', 'seq'))
- new_second_gateup: float32 [2560, 2, 7680], P(('dp', 'seq'), None, 'tensor')
- new_second_down: float32 [7680, 2560], P('tensor', ('dp', 'seq'))
- new_second_scales: float32 [2, 2560], P(None, ('dp', 'seq'))
All inputs are finite; a program needn't handle non-finite values.
Results may differ from a plain program's by a relative error of at most 0.02.
Values may be sent and summed in bfloat16 or wider, within the bound.
A program may use at most 384 MiB of HBM per device.

v0:
```python
import functools

import jax
import jax.numpy as jnp
from jax import lax
from jax.experimental import pallas as pl
from jax.experimental.pallas import tpu as pltpu
from jax.sharding import Mesh
from jax.sharding import PartitionSpec as P

D = 2560
H = 10
HD = 256
FF = 7680
WINDOW = 2048
STEP = 10

eps_norm = 1e-06
masked_fill = -1e30
first_decay = 0.9
second_decay = 0.95
adam_eps = 1e-08
weight_decay = 0.1
gain_rate = 0.2
GELU_SCALE = (2.0 / 3.141592653589793) ** 0.5
GELU_CUBE = 0.044715

MESH = pl.DeviceIdType.MESH
LOW = jnp.bfloat16
F32 = jnp.float32
RING = 4
BLOCK = 160
HALF = BLOCK // 2
PART = 48
OWN = 40
PAD = 48
SPANS = ((0, 48, 32), (48, 32, 16))
MAIN = 896
TAIL = 64


def step(axis, distance):
    return lax.rem(lax.axis_index(axis) + (RING + distance), RING)


def sibling():
    return {"tensor": 1 - lax.axis_index("tensor")}


def greet(peers):
    barrier = pltpu.get_barrier_semaphore()
    for peer in peers:
        pl.semaphore_signal(barrier, inc=1, device_id=peer, device_id_type=MESH)
    pl.semaphore_wait(barrier, len(peers))


def dot(left_side, right_side, contract):
    return lax.dot_general(
        left_side, right_side, ((contract[:1], contract[1:]), ((), ())), preferred_element_type=F32
    )


class Mover:
    def __init__(self, send_sem, recv_sem):
        self.send_sem, self.recv_sem, self.pending = send_sem, recv_sem, []

    def copy(self, src, dst, peer):
        index = len(self.pending)
        one = pltpu.make_async_remote_copy(
            src_ref=src,
            dst_ref=dst,
            send_sem=self.send_sem.at[index],
            recv_sem=self.recv_sem.at[index],
            device_id=peer,
            device_id_type=MESH,
        )
        one.start()
        self.pending.append(one)
        return one

    def finish(self):
        for one in self.pending:
            one.wait_send()


def advance(steps):
    next(steps, None)


def plane_peers(axes):
    return [{axis: step(axis, d)} for axis in axes for d in (-1, 1)]


def exchange_steps(mover, src, dst):
    me = lax.axis_index("z")
    copies = [
        mover.copy(src.at[step("z", d)], dst.at[me], {"z": step("z", d)}) for d in (2, 1, 3)
    ]
    yield
    for copy in copies:
        copy.wait_recv()


def core_rows(lo=0, n=HALF, part=PART):
    base = lax.axis_index("tensor") * HALF

    def rows(start, size):
        return pl.ds(pl.multiple_of(start, 16), size)

    return (
        rows(base + lo, n),
        rows(base + lo, part),
        rows(base + (lo + part), n - part),
        rows(HALF - base + lo, n),
    )


def gather_steps(mover, x, out, span=(0, HALF, PART)):
    me, left, right, far = (step("z", d) for d in (0, -1, 1, 2))
    half, first, last, _ = core_rows(*span)
    to_right = mover.copy(x.at[half], out.at[me, half], {"z": right})
    to_left = mover.copy(x.at[half], out.at[me, half], {"z": left})
    yield
    to_right.wait_recv()
    on_right = mover.copy(out.at[left, first], out.at[left, first], {"z": right})
    shares = [mover.copy(out.at[left, half], out.at[left, half], sibling())]
    to_left.wait_recv()
    on_left = mover.copy(out.at[right, last], out.at[right, last], {"z": left})
    shares.append(mover.copy(out.at[right, half], out.at[right, half], sibling()))
    yield
    on_right.wait_recv()
    on_left.wait_recv()
    shares.append(mover.copy(out.at[far, half], out.at[far, half], sibling()))
    yield
    for copy in shares:
        copy.wait_recv()


def cut_rows(which, cut):
    base, size = (0, cut) if which == 0 else (cut, BLOCK - cut)
    part = -(-size // 32) * 16
    return pl.ds(base, size), pl.ds(base, part), pl.ds(base + part, size - part)


def plane_gather_steps(mover, axes, x, out, cut=HALF, order=(0, 1), share=False):
    a, b = (lax.axis_index(axis) for axis in axes)
    state = {}
    for which, axis in enumerate(axes):
        rows = cut_rows(which, cut)[0]
        place = (lambda i, r: out.at[i, b, r]) if which == 0 else (lambda i, r: out.at[a, i, r])
        me = (a, b)[which]
        to_right = mover.copy(x.at[rows], place(me, rows), {axis: step(axis, 1)})
        to_left = mover.copy(x.at[rows], place(me, rows), {axis: step(axis, -1)})
        state[which] = (axis, place, to_right, to_left)
    yield
    passed = {}
    for which in order:
        axis, place, to_right, to_left = state[which]
        _, first, last = cut_rows(which, cut)
        left, right = step(axis, -1), step(axis, 1)
        to_right.wait_recv()
        on_right = mover.copy(place(left, first), place(left, first), {axis: right})
        to_left.wait_recv()
        on_left = mover.copy(place(right, last), place(right, last), {axis: left})
        passed[which] = (on_right, on_left)
    yield
    state = {}
    shares = []

    def give(piece):
        if share:
            shares.append(mover.copy(piece, piece, sibling()))

    for which in order:
        axis, other = axes[which], axes[1 - which]
        rows = cut_rows(which, cut)[0]
        if which == 0:
            place = lambda i, lo, n, rows=rows: out.at[pl.ds(lo, n), i, rows]
        else:
            place = lambda i, lo, n, rows=rows: out.at[i, pl.ds(lo, n), rows]
        me = (b, a)[which]
        for copy in passed[which]:
            copy.wait_recv()
        to_right = mover.copy(place(me, 0, 4), place(me, 0, 4), {other: step(other, 1)})
        to_left = mover.copy(place(me, 0, 4), place(me, 0, 4), {other: step(other, -1)})
        give(place(me, 0, 4))
        state[which] = (other, place, to_right, to_left)
        yield
    ends = []
    for which in order:
        other, place, to_right, to_left = state[which]
        left, right = step(other, -1), step(other, 1)
        to_right.wait_recv()
        ends.append(mover.copy(place(left, 0, 2), place(left, 0, 2), {other: right}))
        give(place(left, 0, 4))
        to_left.wait_recv()
        ends.append(mover.copy(place(right, 2, 2), place(right, 2, 2), {other: left}))
        give(place(right, 0, 4))
        yield
    for copy in ends:
        copy.wait_recv()
    for which in order:
        other, place, _, _ = state[which]
        give(place(step(other, 2), 0, 4))
    for copy in shares:
        copy.wait_recv()


def lanes(shape):
    return lax.broadcasted_iota(jnp.int32, shape, len(shape) - 1)


def turn(values, cos, sin):
    return values * cos + pltpu.roll(values, 64, 1) * sin


def whole_rows(blocks, stage, dst):
    for i in range(RING):
        stage[i * OWN : (i + 1) * OWN] = blocks[i].astype(F32)[:OWN]
    dst[...] = stage[...].astype(LOW)


def first_kernel(
    w_query,
    w_keyvalue,
    w_out,
    w_gateup,
    w_down,
    scale_columns,
    tokens,
    cotangent,
    cos_ref,
    sin_ref,
    cos_kv,
    sin_kv,
    feed_full,
    attn_a,
    attn_b,
    normed_one,
    dy_all,
    query,
    kv_out,
    log_total,
    att_slice,
    residual,
    normed_two,
    attended,
    gain_ref,
    attn_rows,
    feed_rows,
    send_sem,
    recv_sem,
    local_sem,
    cot_in,
    dy,
    attn_got,
    mine_a,
    mine_b,
    weight_a,
    weight_b,
    attn_stage,
    feed_got,
    feed_mine,
    feed_stage,
    unit_low,
    unit_all,
    normed,
    qkv_send,
    qkv_got,
    kv_own,
    keyvalue,
    scores,
    att_send,
    part,
    sum_half,
    normed_low,
    *bufs,
):
    z, x, y, core = (lax.axis_index(axis) for axis in ("z", "x", "dp", "tensor"))
    plane = ("dp", "x")
    saves = []

    def save(src, dst):
        saves.append(pltpu.make_async_copy(src, dst, local_sem.at[len(saves)]))
        saves[-1].start()
        return saves[-1]

    cot_load = pltpu.make_async_copy(cotangent, cot_in, local_sem.at[15])
    cot_load.start()
    low = lanes((OWN, 128)) < TAIL

    def put(rows, j, lo, values):
        padding = jnp.zeros((PAD - OWN, values.shape[1]), F32)
        rows[j, :, lo : lo + values.shape[1]] = jnp.concatenate([values, padding]).astype(LOW)

    def pair(one, two, odd):
        if odd:
            return jnp.where(low, pltpu.roll(one, TAIL, 1), two)
        return jnp.where(low, one, pltpu.roll(two, TAIL, 1))

    for j in range(RING):
        head = slice(HD * j, HD * (j + 1))
        tile = slice((j // 2) * 128, (j // 2 + 1) * 128)
        last = slice(4 * HD + tile.start, 4 * HD + tile.stop)
        kv_tile = jnp.where(core == 0, w_keyvalue[:, 0, tile], w_keyvalue[:, 1, tile])
        out_tile = pltpu.roll(w_out[:, last], TAIL, 1) if j % 2 else w_out[:, last]
        put(attn_rows, j, 0, w_query[:, head])
        put(attn_rows, j, HD, pair(w_query[:, last], kv_tile, j % 2))
        put(attn_rows, j, 384, jnp.where(low, out_tile, scale_columns[...]))
        put(attn_rows, j, 512, w_out[:, head])
    greet([{"z": step("z", d)} for d in (1, 2, 3)] + plane_peers(plane) + [sibling()])
    mover = Mover(send_sem, recv_sem)

    attn_swap = exchange_steps(mover, attn_rows, attn_got)
    advance(attn_swap)
    for j in range(RING):
        main = slice(MAIN * j, MAIN * (j + 1))
        last = slice(RING * MAIN + (j // 2) * 128, RING * MAIN + (j // 2 + 1) * 128)
        down_tile = pltpu.roll(w_down[:, last], TAIL, 1) if j % 2 else w_down[:, last]
        put(feed_rows, j, 0, w_gateup[:, 0, main])
        put(feed_rows, j, MAIN, w_gateup[:, 1, main])
        put(feed_rows, j, 2 * MAIN, pair(w_gateup[:, 0, last], w_gateup[:, 1, last], j % 2))
        put(feed_rows, j, 2 * (MAIN + TAIL), w_down[:, main])
        put(feed_rows, j, 3 * MAIN + 2 * TAIL, jnp.where(low, down_tile, 0.0))
    feed_swap = exchange_steps(mover, feed_rows, feed_got)
    advance(feed_swap)
    values = tokens[...]
    unit = values * lax.rsqrt(jnp.mean(values * values, axis=-1, keepdims=True) + eps_norm)
    unit_low[...] = unit.astype(LOW)
    unit_gather = gather_steps(mover, unit_low, unit_all)
    advance(unit_gather)
    attn_got[z] = attn_rows[z]
    advance(attn_swap)
    for i in range(RING):
        attn_stage[i * OWN : (i + 1) * OWN] = attn_got[i].astype(F32)[:OWN]
    mine_a[...] = attn_stage[:, :512].astype(LOW)
    mine_b[...] = attn_stage[:, 512:].astype(LOW)
    a_gather = plane_gather_steps(mover, plane, mine_a, weight_a)
    advance(a_gather)
    weight_a[y, x] = mine_a[...]
    unit_all[z] = unit_low[...]
    advance(a_gather)
    feed_got[z] = feed_rows[z]
    advance(a_gather)
    advance(a_gather)
    advance(feed_swap)
    whole_rows(feed_got, feed_stage, feed_mine)
    feed_own = save(feed_mine, feed_full.at[y, x])
    advance(unit_gather)
    advance(a_gather)
    advance(a_gather)
    feed_gather = plane_gather_steps(mover, plane, feed_mine, feed_full)
    advance(feed_gather)
    advance(unit_gather)
    advance(unit_gather)
    advance(a_gather)
    save(weight_a, attn_a)

    scale_cols = weight_a[:, :, :, 384:].reshape(D, 128)
    pick = (lanes((8, 128)) == TAIL + lax.broadcasted_iota(jnp.int32, (8, 128), 0)).astype(LOW)
    gain_ref[...] = 1.0 + dot(pick, scale_cols, (1, 1))
    qkv_weight = weight_a[:, :, :, :384].reshape(D, 384)
    copies = []
    for d in (2, 1, 3, 0):
        block = step("z", d)
        rows = (unit_all[block].astype(F32) * gain_ref[0:1, :]).astype(LOW)
        normed[block] = rows
        qkv_send[block] = dot(rows, qkv_weight, (1, 0)).astype(LOW)
        if d:
            copies.append(mover.copy(qkv_send.at[block], qkv_got.at[z], {"z": block}))
    save(normed, normed_one)
    qkv_got[z] = qkv_send[z]
    feed_own.wait()
    advance(feed_gather)
    for copy in copies:
        copy.wait_recv()
    low_lanes = lanes((BLOCK, 128)) < TAIL
    cos, sin = cos_ref[...], sin_ref[...]

    def joined(i, offset):
        one, two = (qkv_got[i + k, :, 256:384].astype(F32) for k in (0, 1))
        if offset == 0:
            return jnp.where(low_lanes, one, pltpu.roll(two, TAIL, 1))
        return jnp.where(low_lanes, pltpu.roll(one, TAIL, 1), two)

    kv_own[:, :128] = turn(joined(0, 1), cos_kv[...], sin_kv[...]).astype(LOW)
    kv_own[:, 128:] = joined(2, 1).astype(LOW)
    kv_mine = keyvalue.at[core]
    kv_gather = plane_gather_steps(mover, ("x", "z"), kv_own, kv_mine, share=True)
    advance(kv_gather)
    keyvalue[core, x, z] = kv_own[...]
    scale = HD ** (-0.5)
    for h in range(4):
        first = qkv_got[h, :, :128].astype(F32)
        query[h, :, :128] = (turn(first, cos, sin) * scale).astype(LOW)
        query[h, :, 128:] = (qkv_got[h, :, 128:256].astype(F32) * scale).astype(LOW)
    query[4, :, :128] = (turn(joined(0, 0), cos, sin) * scale).astype(LOW)
    query[4, :, 128:] = (joined(2, 0) * scale).astype(LOW)
    b_gather = plane_gather_steps(mover, plane, mine_b, weight_b)
    advance(b_gather)
    weight_b[y, x] = mine_b[...]
    advance(kv_gather)
    advance(b_gather)
    for _ in range(2):
        advance(kv_gather)
        advance(b_gather)
    for _ in range(2):
        advance(kv_gather)
        advance(b_gather)
    for _ in range(2):
        advance(feed_gather)
    cot_load.wait()
    dy[...] = cot_in[...].astype(LOW)
    dy_gather = gather_steps(mover, dy, dy_all)
    advance(dy_gather)
    save(dy, dy_all.at[z])
    advance(kv_gather)
    save(keyvalue, kv_out)

    start = (x * RING + z) * BLOCK
    chunk = RING * BLOCK

    def one_head(h, carry):
        queries = query[h]
        top = jnp.full((BLOCK, 1), masked_fill, F32)
        for k in range(RING):
            rows = keyvalue[0, k].reshape(chunk, HD)
            tile = dot(queries, rows, (1, 1))
            gap = (start - k * chunk) + (
                lax.broadcasted_iota(jnp.int32, tile.shape, 0) - lanes(tile.shape)
            )
            tile = jnp.where((gap >= 0) & (gap < WINDOW), tile, masked_fill)
            scores[:, k * chunk : (k + 1) * chunk] = tile
            top = jnp.maximum(top, jnp.max(tile, axis=-1, keepdims=True))
        sums = jnp.zeros((BLOCK, 1), F32)
        for k in range(RING):
            tile = jnp.exp(scores[:, k * chunk : (k + 1) * chunk] - top)
            scores[:, k * chunk : (k + 1) * chunk] = tile
            sums = sums + jnp.sum(tile, axis=-1, keepdims=True)
        inverse = 1.0 / sums
        result = jnp.zeros((BLOCK, HD), F32)
        for k in range(RING):
            low = (scores[:, k * chunk : (k + 1) * chunk] * inverse).astype(LOW)
            result = result + dot(low, keyvalue[1, k].reshape(chunk, HD), (1, 0))
        attended[h] = result
        log_total[h] = jnp.broadcast_to(top + jnp.log(sums), (BLOCK, 128))
        return carry

    lax.fori_loop(0, 5, one_head, 0)
    for j in range(RING):
        att_send[j, :, 128:] = attended[j].astype(LOW)
        tile = attended[4, :, (j // 2) * 128 : (j // 2 + 1) * 128]
        tile = pltpu.roll(tile, TAIL, 1) if j % 2 else tile
        att_send[j, :, :128] = jnp.where(low_lanes, tile, 0.0).astype(LOW)
    att_swap = exchange_steps(mover, att_send, att_slice)
    advance(att_swap)
    att_slice[z] = att_send[z]
    advance(att_swap)

    advance(b_gather)
    save(weight_b, attn_b)

    last_weight = weight_a[:, :, :, 384:].reshape(D, 128)
    main_weight = weight_b[...].reshape(D, HD)

    def make(block):
        rows = dot(att_slice[block, :, :128], last_weight, (1, 1))
        part[block] = (rows + dot(att_slice[block, :, 128:], main_weight, (1, 1))).astype(LOW)

    shares = []
    sharing = share_steps(mover, part, bufs[0], shares, make)
    advance(sharing)
    advance(sharing)
    sums = [
        reduce_steps(mover, own_rows(part), shares[i], bufs, sum_half, span)
        for i, span in enumerate(SPANS)
    ]
    for one in sums:
        advance(one)
    advance(sharing)
    advance(sharing)
    for one in sums:
        advance(one)

    def normed_rows(rows):
        unit = rows * lax.rsqrt(jnp.mean(rows * rows, axis=-1, keepdims=True) + eps_norm)
        return (unit * gain_ref[1:2, :]).astype(LOW)

    gathers, res_shares = [], []
    for one, span in zip(sums, SPANS, strict=True):
        advance(one)
        place = core_rows(*span)[0]
        rows = tokens[place, :] + sum_half[span[0] : span[0] + span[1]]
        residual[place, :] = rows
        normed_low[place, :] = normed_rows(rows)
        gathers.append(gather_steps(mover, normed_low, normed_two, span))
        advance(gathers[-1])
        res_shares.append(mover.copy(residual.at[place], residual.at[place], sibling()))
    advance(dy_gather)
    for copy in res_shares:
        copy.wait_recv()
    theirs = core_rows()[3]
    normed_low[theirs, :] = normed_rows(residual[theirs, :])
    save(normed_low, normed_two.at[z])
    for one in gathers:
        advance(one)
    advance(feed_gather)
    advance(feed_gather)
    for one in gathers:
        advance(one)
    advance(dy_gather)
    for one in gathers:
        advance(one)
    advance(dy_gather)
    advance(feed_gather)
    for one in saves:
        if one is not feed_own:
            one.wait()
    mover.finish()


def run_first(*operands):
    out = {
        "feed_full": ((RING, RING, BLOCK, 2944), LOW),
        "attn_a": ((RING, RING, BLOCK, 512), LOW),
        "attn_b": ((RING, RING, BLOCK, HD), LOW),
        "normed_one": ((RING, BLOCK, D), LOW),
        "dy_all": ((RING, BLOCK, D), LOW),
        "query": ((5, BLOCK, HD), LOW),
        "keyvalue": ((2, RING, RING, BLOCK, HD), LOW),
        "log_total": ((5, BLOCK, 128), F32),
        "att_slice": ((RING, BLOCK, 384), LOW),
        "residual": ((BLOCK, D), F32),
        "normed_two": ((RING, BLOCK, D), LOW),
        "attended": ((5, BLOCK, HD), F32),
        "gains": ((8, D), F32),
        "attn_rows": ((RING, PAD, 768), LOW),
        "feed_rows": ((RING, PAD, 2944), LOW),
    }
    remote = ("feed_full", "attn_a", "attn_b", "normed_one", "dy_all", "keyvalue", "normed_two")
    spaces = [pltpu.VMEM] * 7 + [pl.ANY] + [pltpu.VMEM] * 4
    scratch = [
        pltpu.VMEM((BLOCK, D), F32),
        pltpu.VMEM((BLOCK, D), LOW),
        pltpu.VMEM((RING, PAD, 768), LOW),
        pltpu.VMEM((BLOCK, 512), LOW),
        pltpu.VMEM((BLOCK, HD), LOW),
        pltpu.VMEM((RING, RING, BLOCK, 512), LOW),
        pltpu.VMEM((RING, RING, BLOCK, HD), LOW),
        pltpu.VMEM((BLOCK, 768), F32),
        pltpu.VMEM((RING, PAD, 2944), LOW),
        pltpu.VMEM((BLOCK, 2944), LOW),
        pltpu.VMEM((BLOCK, 2944), F32),
        pltpu.VMEM((BLOCK, D), LOW),
        pltpu.VMEM((RING, BLOCK, D), LOW),
        pltpu.VMEM((RING, BLOCK, D), LOW),
        pltpu.VMEM((RING, BLOCK, 384), LOW),
        pltpu.VMEM((RING, BLOCK, 384), LOW),
        pltpu.VMEM((BLOCK, HD), LOW),
        pltpu.VMEM((2, RING, RING, BLOCK, HD), LOW),
        pltpu.VMEM((BLOCK, RING * RING * BLOCK), F32),
        pltpu.VMEM((RING, BLOCK, 384), LOW),
        pltpu.VMEM((RING, BLOCK, D), LOW),
        pltpu.VMEM((HALF, D), F32),
        pltpu.VMEM((BLOCK, D), LOW),
        *reduce_scratch(),
    ]
    return call(
        first_kernel, 1, 150, out, scratch, operands, spaces, {name: pl.ANY for name in remote}
    )


def plane_reduce_steps(mover, axes, g, bufs, res, loads=None):
    far, side, near, far_two, side_two = bufs
    places = [lax.axis_index(axis) for axis in axes]

    def block(which, i, lo, n):
        rows = pl.ds(which * HALF, HALF)
        return g.at[i, pl.ds(lo, n), rows] if which == 0 else g.at[pl.ds(lo, n), i, rows]

    locals_ = []

    def load(src, dst):
        locals_.append(pltpu.make_async_copy(src, dst, loads.at[len(locals_)]))
        locals_[-1].start()
        return locals_[-1]

    first, sides, wanted = [], [], []
    for which, axis in enumerate(axes):
        right, left = step(axis, 1), step(axis, -1)
        far_place = step(axis, 2)
        first.append(
            (
                mover.copy(block(which, far_place, 0, 2), far.at[which, pl.ds(0, 2)], {axis: right}),
                mover.copy(block(which, far_place, 2, 2), far.at[which, pl.ds(2, 2)], {axis: left}),
            )
        )
        if loads is not None:
            wanted.append(
                (
                    load(block(which, right, 0, 2), near.at[which, 0]),
                    load(block(which, left, 2, 2), near.at[which, 1]),
                )
            )
    for which, axis in enumerate(axes):
        right, left = step(axis, 1), step(axis, -1)
        sides.append(
            [
                mover.copy(block(which, right, 2, 2), side.at[which, 0, pl.ds(2, 2)], {axis: right}),
                mover.copy(block(which, left, 0, 2), side.at[which, 1, pl.ds(0, 2)], {axis: left}),
            ]
        )
    yield
    owned = []
    for which, axis in enumerate(axes):
        for k, (d, lo) in enumerate(((1, 0), (-1, 2))):
            first[which][k].wait_recv()
            if loads is not None:
                wanted[which][k].wait()
                term = near[which, k]
            else:
                term = block(which, step(axis, d), lo, 2)[...]
            near[which, k] = (term.astype(F32) + far[which, lo : lo + 2].astype(F32)).astype(LOW)
            sides[which].append(
                mover.copy(near.at[which, k], side.at[which, k, pl.ds(lo, 2)], {axis: step(axis, d)})
            )
        if loads is not None:
            owned.append(load(block(which, places[which], 0, 4), far.at[which]))
    yield

    def summed(which, i):
        if loads is not None:
            term = far[which, i]
        else:
            rows = pl.ds(which * HALF, HALF)
            me = places[which]
            term = (g[me, i, rows] if which == 0 else g[i, me, rows])
        return (
            term.astype(F32) + side[which, 0, i].astype(F32) + side[which, 1, i].astype(F32)
        )

    second = []
    for which, axis in enumerate(axes):
        other = axes[1 - which]
        right, left = {other: step(other, 1)}, {other: step(other, -1)}
        for copy in sides[which]:
            copy.wait_recv()
        if loads is not None:
            owned[which].wait()
        far_two[which, 0] = summed(which, step(other, 2)).astype(LOW)
        upper, lower = pl.ds(0, PART), pl.ds(PART, HALF - PART)
        second.append(
            (
                mover.copy(far_two.at[which, 0, upper], far_two.at[which, 1, upper], right),
                mover.copy(far_two.at[which, 0, lower], far_two.at[which, 1, lower], left),
            )
        )
    yield
    last = []
    for which, axis in enumerate(axes):
        other = axes[1 - which]
        right, left = step(other, 1), step(other, -1)
        total = summed(which, right)
        second[which][0].wait_recv()
        side_two[which, 0, :PART] = (
            total[:PART] + far_two[which, 1, :PART].astype(F32)
        ).astype(LOW)
        side_two[which, 0, PART:] = total[PART:].astype(LOW)
        last.append(mover.copy(side_two.at[which, 0], side_two.at[which, 2], {other: right}))
        total = summed(which, left)
        second[which][1].wait_recv()
        side_two[which, 1, :PART] = total[:PART].astype(LOW)
        side_two[which, 1, PART:] = (
            total[PART:] + far_two[which, 1, PART:].astype(F32)
        ).astype(LOW)
        last.append(mover.copy(side_two.at[which, 1], side_two.at[which, 3], {other: left}))
    yield
    for which, axis in enumerate(axes):
        other = axes[1 - which]
        last[2 * which].wait_recv()
        last[2 * which + 1].wait_recv()
        res[which * HALF : (which + 1) * HALF] = (
            summed(which, lax.axis_index(other))
            + side_two[which, 2].astype(F32)
            + side_two[which, 3].astype(F32)
        )


def plane_reduce_scratch(columns):
    return [
        pltpu.VMEM((2, 4, HALF, columns), LOW),
        pltpu.VMEM((2, 2, 4, HALF, columns), LOW),
        pltpu.VMEM((2, 2, 2, HALF, columns), LOW),
        pltpu.VMEM((2, 2, HALF, columns), LOW),
        pltpu.VMEM((2, 4, HALF, columns), LOW),
        pltpu.VMEM((BLOCK, columns), F32),
    ]


def share_steps(mover, part, other, shares, make=None, spans=SPANS):
    me, left, right, far = (step("z", d) for d in (0, -1, 1, 2))
    shares.extend([] for _ in spans)
    for slot, block in enumerate((far, right, left, me)):
        if make is not None:
            make(block)
        for copies, (lo, n, first) in zip(shares, spans, strict=True):
            theirs = core_rows(lo, n, first)[3]
            copies.append(
                mover.copy(part.at[block, theirs], other.at[slot, pl.ds(lo, n)], sibling())
            )
        yield


def reduce_steps(mover, mine, shares, bufs, out, span):
    other, total, far_in, from_left, from_right = bufs
    lo, n, part = span
    me, left, right, far = (step("z", d) for d in (0, -1, 1, 2))
    blocks = (far, right, left, me)
    rows, first, last = pl.ds(lo, n), pl.ds(lo, part), pl.ds(lo + part, n - part)

    def both(slot):
        return mine(blocks[slot], span).astype(F32) + other[slot, rows].astype(F32)

    shares[0].wait_recv()
    total[0, rows] = both(0).astype(LOW)
    far_right = mover.copy(total.at[0, first], far_in.at[first], {"z": right})
    far_left = mover.copy(total.at[0, last], far_in.at[last], {"z": left})
    yield
    shares[1].wait_recv()
    summed = both(1)
    far_right.wait_recv()
    total[1, first] = (summed[:part] + far_in[first].astype(F32)).astype(LOW)
    total[1, last] = summed[part:].astype(LOW)
    to_right = mover.copy(total.at[1, rows], from_left.at[rows], {"z": right})
    shares[2].wait_recv()
    summed = both(2)
    far_left.wait_recv()
    total[2, first] = summed[:part].astype(LOW)
    total[2, last] = (summed[part:] + far_in[last].astype(F32)).astype(LOW)
    to_left = mover.copy(total.at[2, rows], from_right.at[rows], {"z": left})
    yield
    shares[3].wait_recv()
    summed = both(3)
    to_right.wait_recv()
    to_left.wait_recv()
    out[rows] = summed + from_left[rows].astype(F32) + from_right[rows].astype(F32)


def own_rows(ref):
    return lambda block, span: ref[block, core_rows(*span)[0]]


def half_rows(ref):
    return lambda block, span: ref[block, pl.ds(span[0], span[1])]


def reduce_scratch():
    return [
        pltpu.VMEM((4, HALF, D), LOW),
        pltpu.VMEM((3, HALF, D), LOW),
        pltpu.VMEM((HALF, D), LOW),
        pltpu.VMEM((HALF, D), LOW),
        pltpu.VMEM((HALF, D), LOW),
    ]


def spread_rows(res, dst):
    for i in range(RING):
        rows = res[i * OWN : (i + 1) * OWN]
        dst[i] = jnp.concatenate([rows, jnp.zeros((PAD - OWN, rows.shape[1]), F32)]).astype(LOW)


def activation(gate, upper, grad):
    square = gate * gate
    tanh = jnp.tanh(GELU_SCALE * gate * (1.0 + GELU_CUBE * square))
    half = 0.5 * (1.0 + tanh)
    gelu = gate * half
    slope = half + 0.5 * gate * (1.0 - tanh * tanh) * GELU_SCALE * (1.0 + 3.0 * GELU_CUBE * square)
    return gelu * upper, grad * upper * slope, grad * gelu


def second_kernel(
    feed_full,
    normed_two,
    dy_all,
    cotangent,
    residual,
    gain_ref,
    grad_rows,
    da_all,
    feed_part,
    gateup_grads,
    down_rows,
    send_sem,
    recv_sem,
    local_sem,
    normed_in,
    dy_in,
    gateup_weight,
    down_weight,
    hidden,
    dgu,
    norm_part,
    stage,
    grad_half,
    cot_half,
    res_half,
    da_low,
    *bufs,
):
    z = lax.axis_index("z")
    half, _, _, _ = core_rows()
    plane = ("dp", "x")
    gu_width = 2 * (MAIN + TAIL)
    wide = RING * BLOCK
    loads = [
        pltpu.make_async_copy(src, dst, local_sem.at[i])
        for i, (src, dst) in enumerate(
            (
                (normed_two, normed_in),
                (feed_full.at[:, :, :, pl.ds(0, gu_width)], gateup_weight),
                (dy_all, dy_in),
                (feed_full.at[:, :, :, pl.ds(gu_width, 1024)], down_weight),
                (cotangent.at[half], cot_half),
                (residual.at[half], res_half),
            )
        )
    ]
    for load in loads:
        load.start()
    greet(plane_peers(("z",)) + plane_peers(plane) + [sibling()])
    mover = Mover(send_sem, recv_sem)
    for load in loads:
        load.wait()

    def product(rows, weight, lo, n):
        left_side = rows[...].reshape(wide, D)
        return dot(left_side, weight[:, :, :, lo : lo + n].reshape(D, n), (1, 0))

    for lo, n in ((0, 256), (256, 256), (512, 256), (768, 128)):
        value, grad_gate, grad_upper = activation(
            product(normed_in, gateup_weight, lo, n),
            product(normed_in, gateup_weight, MAIN + lo, n),
            product(dy_in, down_weight, lo, n),
        )
        hidden[:, lo : lo + n] = value.astype(LOW)
        dgu[:, lo : lo + n] = grad_gate.astype(LOW)
        dgu[:, MAIN + lo : MAIN + lo + n] = grad_upper.astype(LOW)
    both = product(normed_in, gateup_weight, 2 * MAIN, 2 * TAIL)
    value, grad_gate, grad_upper = activation(
        both, pltpu.roll(both, TAIL, 1), product(dy_in, down_weight, MAIN, 2 * TAIL)
    )
    low_lanes = lanes(both.shape) < TAIL
    hidden[:, MAIN:] = jnp.where(low_lanes, value, 0.0).astype(LOW)
    dgu[:, 2 * MAIN :] = jnp.where(low_lanes, grad_gate, pltpu.roll(grad_upper, TAIL, 1)).astype(LOW)

    for i in range(RING):
        part = dot(dgu[...], gateup_weight[i].reshape(wide, gu_width), (1, 1))
        norm_part[:, :, i * wide : (i + 1) * wide] = part.astype(LOW).reshape(RING, BLOCK, wide)
    shares = []
    sharing = share_steps(mover, norm_part, bufs[0], shares)
    for _ in range(RING):
        advance(sharing)
    sums = [
        reduce_steps(mover, own_rows(norm_part), shares[i], bufs[:5], grad_half, span)
        for i, span in enumerate(SPANS)
    ]

    for i in range(RING):
        terms = dot(hidden[...], down_weight[i].reshape(wide, 1024), (1, 1))
        feed_part[:, :, i * wide : (i + 1) * wide] = terms.astype(LOW).reshape(RING, BLOCK, wide)
        if i < 2:
            advance(sums[i])

    def columns(rows, i):
        return rows[:, :, i * wide : (i + 1) * wide].reshape(wide, wide)

    for i in range(RING):
        grads = dot(columns(dy_in, i), hidden[...], (0, 0))
        down_weight[i] = grads.astype(LOW).reshape(RING, BLOCK, 1024)
        if i < 2:
            advance(sums[i])
    down_sum = plane_reduce_steps(mover, plane, down_weight, bufs[5:10], bufs[10])
    advance(down_sum)
    saved = []

    def gateup_block(i):
        if saved:
            saved[-1].wait()
        grads = dot(columns(normed_in, i), dgu[...], (0, 0))
        stage[...] = grads.astype(LOW).reshape(RING, BLOCK, gu_width)
        saved.append(pltpu.make_async_copy(stage, gateup_grads.at[i], local_sem.at[10 + i]))
        saved[-1].start()

    gateup_block(0)
    gathers, da_shares = [], []
    for one, span in zip(sums, SPANS, strict=True):
        advance(one)
        piece = pl.ds(span[0], span[1])
        place = core_rows(*span)[0]
        rows = res_half[piece, :]
        inverse = lax.rsqrt(jnp.mean(rows * rows, axis=-1, keepdims=True) + eps_norm)
        unit = rows * inverse
        scaled = grad_half[piece, :] * gain_ref[1:2, :]
        grad = cot_half[piece, :] + inverse * (
            scaled - unit * jnp.mean(scaled * unit, axis=-1, keepdims=True)
        )
        grad_rows[piece, :] = grad
        da_low[place, :] = grad.astype(LOW)
        gathers.append(gather_steps(mover, da_low, da_all, span))
        advance(gathers[-1])
        da_shares.append(mover.copy(da_low.at[place], da_low.at[place], sibling()))
    advance(down_sum)
    gateup_block(1)
    for copy in da_shares:
        copy.wait_recv()
    da_own = pltpu.make_async_copy(da_low, da_all.at[z], local_sem.at[9])
    da_own.start()
    for one in gathers:
        advance(one)
    gateup_block(2)
    advance(down_sum)
    for one in gathers:
        advance(one)
    gateup_block(3)
    advance(down_sum)
    for one in gathers:
        advance(one)
    advance(down_sum)
    spread_rows(bufs[10], down_rows)
    saved[-1].wait()
    da_own.wait()
    mover.finish()


def third_kernel(
    feed_part,
    gateup_grads,
    da_all,
    residual,
    attn_a,
    attn_b,
    att_slice,
    query,
    kv_hbm,
    log_total,
    attended,
    cos_ref,
    sin_ref,
    cos_kv,
    sin_kv,
    grad_out,
    grad_got,
    gateup_rows,
    output,
    send_sem,
    recv_sem,
    local_sem,
    da_in,
    last_weight,
    main_weight,
    keyvalue,
    feed_mine,
    out_half,
    datt_send,
    datt_got,
    datt,
    delta,
    ds_all,
    p_all,
    dq,
    kv_pair,
    kv_in,
    grad_kv,
    grad_query,
    grad_send,
    kv_low,
    *bufs,
):
    z, core = lax.axis_index("z"), lax.axis_index("tensor")
    x = lax.axis_index("x")
    half = core_rows()[0]
    whole_span = ((0, HALF, PART),)
    out_bufs, rows_bufs, rows_res = bufs[:5], bufs[5:10], bufs[10]
    kv_bufs, kv_rows = bufs[11:16], bufs[16]
    loads = [
        pltpu.make_async_copy(src, dst, local_sem.at[8 + i])
        for i, (src, dst) in enumerate(
            (
                (da_all, da_in),
                (attn_a.at[:, :, :, pl.ds(384, 128)], last_weight),
                (attn_b, main_weight),
                (kv_hbm, keyvalue),
                (feed_part.at[:, half], feed_mine),
            )
        )
    ]
    for load in loads:
        load.start()
    greet([{"z": step("z", d)} for d in (1, 2, 3)] + plane_peers(("dp", "x")) + [sibling()])
    mover = Mover(send_sem, recv_sem)
    rows_sum = plane_reduce_steps(
        mover, ("dp", "x"), gateup_grads, rows_bufs, rows_res, loads=local_sem
    )
    advance(rows_sum)
    for load in loads[:3]:
        load.wait()
    last = last_weight[...].reshape(D, 128)
    main = main_weight[...].reshape(D, HD)
    copies = []
    for d in (2, 1, 3, 0):
        block = step("z", d)
        datt_send[block, :, :128] = dot(da_in[block], last, (1, 0)).astype(LOW)
        datt_send[block, :, 128:] = dot(da_in[block], main, (1, 0)).astype(LOW)
        if d:
            copies.append(mover.copy(datt_send.at[block], datt_got.at[z], {"z": block}))
    datt_got[z] = datt_send[z]
    shares = []
    sharing = share_steps(mover, feed_part, out_bufs[0], shares, spans=whole_span)
    for _ in range(RING):
        advance(sharing)
    feed_sum = reduce_steps(
        mover, half_rows(feed_mine), shares[0], out_bufs, out_half, whole_span[0]
    )
    slices = att_slice[...].reshape(RING * BLOCK, 384)
    wide = RING * BLOCK
    for i in range(RING):
        left_side = da_in[:, :, i * wide : (i + 1) * wide].reshape(wide, wide)
        grad_out[i] = dot(left_side, slices, (0, 0)).astype(LOW).reshape(RING, BLOCK, 384)
    for copy in copies:
        copy.wait_recv()
    for load in loads[3:]:
        load.wait()
    advance(feed_sum)
    advance(rows_sum)

    low_lanes = lanes((BLOCK, 128)) < TAIL
    for h in range(4):
        datt[h] = datt_got[h, :, 128:]
    for k in range(2):
        one, two = (datt_got[2 * k + i, :, :128].astype(F32) for i in range(2))
        datt[4, :, k * 128 : (k + 1) * 128] = jnp.where(
            low_lanes, one, pltpu.roll(two, TAIL, 1)
        ).astype(LOW)
    for h in range(5):
        delta[h] = jnp.broadcast_to(
            jnp.sum(datt[h].astype(F32) * attended[h], axis=-1, keepdims=True), (BLOCK, 128)
        )
        dq[h] = jnp.zeros((BLOCK, HD), F32)
    start = (x * RING + z) * BLOCK
    chunk = RING * BLOCK

    def one_chunk(k, carry):
        keys = keyvalue[0, k].reshape(chunk, HD)
        values = keyvalue[1, k].reshape(chunk, HD)
        shape = (BLOCK, chunk)
        gap = (start - k * chunk) + (lax.broadcasted_iota(jnp.int32, shape, 0) - lanes(shape))
        visible = (gap >= 0) & (gap < WINDOW)

        def one_head(h, carry):
            scores = dot(query[h], keys, (1, 1))
            probs = jnp.where(visible, jnp.exp(scores - log_total[h, :, :1]), 0.0)
            grads = dot(datt[h], values, (1, 1))
            low = (probs * (grads - delta[h, :, :1])).astype(LOW)
            ds_all[h] = low
            p_all[h] = probs.astype(LOW)
            dq[h] = dq[h] + dot(low, keys, (1, 0))
            return carry

        lax.fori_loop(0, 5, one_head, 0)
        queries = query[...].reshape(5 * BLOCK, HD)
        outer = datt[...].reshape(5 * BLOCK, HD)
        kv_pair[0, k] = dot(ds_all[...].reshape(5 * BLOCK, chunk), queries, (0, 0)).astype(LOW).reshape(RING, BLOCK, HD)
        kv_pair[1, k] = dot(p_all[...].reshape(5 * BLOCK, chunk), outer, (0, 0)).astype(LOW).reshape(RING, BLOCK, HD)
        return carry

    lax.fori_loop(0, RING, one_chunk, 0)
    kv_swap = mover.copy(kv_pair.at[1 - core], kv_in, sibling())
    advance(feed_sum)
    cos, sin = cos_ref[...], sin_ref[...]
    scale = HD ** (-0.5)
    for h in range(5):
        grad_query[h, :, :128] = turn(dq[h, :, :128] * scale, cos, -sin)
        grad_query[h, :, 128:] = dq[h, :, 128:] * scale
    kv_swap.wait_recv()
    grad_kv[...] = (kv_pair[core].astype(F32) + kv_in[...].astype(F32)).astype(LOW)
    kv_sum = plane_reduce_steps(mover, ("x", "z"), grad_kv, kv_bufs, kv_rows)
    advance(kv_sum)
    for h in range(4):
        grad_send[h, :, :HD] = grad_query[h].astype(LOW)
    advance(kv_sum)
    advance(kv_sum)
    advance(kv_sum)
    advance(kv_sum)
    kv_low[:, :128] = turn(kv_rows[:, :128], cos_kv[...], -sin_kv[...])
    kv_low[:, 128:] = kv_rows[:, 128:]
    for j in range(RING):
        place = slice((j // 2) * 128, (j // 2 + 1) * 128)
        one, two = grad_query[4, :, place], kv_low[:, place]
        if j % 2:
            one = pltpu.roll(one, TAIL, 1)
        else:
            two = pltpu.roll(two, TAIL, 1)
        grad_send[j, :, HD:] = jnp.where(low_lanes, one, two).astype(LOW)
    swap = exchange_steps(mover, grad_send, grad_got)
    advance(swap)
    grad_got[z] = grad_send[z]
    advance(feed_sum)
    output[half, :] = residual[half, :] + out_half[...]
    out_share = mover.copy(output.at[half], output.at[half], sibling())
    advance(rows_sum)
    advance(swap)
    advance(rows_sum)
    advance(rows_sum)
    spread_rows(rows_res, gateup_rows)
    out_share.wait_recv()
    mover.finish()


def fourth_kernel(
    grad_got,
    gateup_rows,
    down_rows,
    grad_out,
    attn_a,
    normed_hbm,
    grad_rows,
    tokens,
    gain_ref,
    attn_rows,
    feed_rows,
    grad_tokens,
    gateup_got,
    down_got,
    out_got,
    qkv_got,
    kv_other,
    scale_sums,
    send_sem,
    recv_sem,
    local_sem,
    qkv_weight,
    normed_one,
    part,
    grad_half,
    grad_qkv,
    out_send,
    qkv_send,
    scale_own,
    scale_other,
    *bufs,
):
    z = lax.axis_index("z")
    half, _, _, _ = core_rows()
    plane = ("dp", "x")
    sum_bufs = bufs[:5]
    out_bufs, qkv_bufs = bufs[5:11], bufs[11:17]
    loads = [
        pltpu.make_async_copy(attn_a.at[:, :, :, pl.ds(0, 384)], qkv_weight, local_sem.at[0]),
        pltpu.make_async_copy(normed_hbm, normed_one, local_sem.at[1]),
    ]
    for load in loads:
        load.start()
    greet([{"z": step("z", d)} for d in (1, 2, 3)] + plane_peers(plane) + [sibling()])
    mover = Mover(send_sem, recv_sem)
    out_sum = plane_reduce_steps(mover, plane, grad_out, out_bufs[:5], out_bufs[5])
    advance(out_sum)
    slices = grad_got[...].reshape(RING * BLOCK, 384)
    wide = RING * BLOCK
    loads[0].wait()
    weight = qkv_weight[...].reshape(D, 384)

    def make(block):
        part[block] = dot(grad_got[block], weight, (1, 1)).astype(LOW)

    shares = []
    sharing = share_steps(mover, part, sum_bufs[0], shares, make)
    advance(sharing)
    advance(sharing)
    sums = [
        reduce_steps(mover, own_rows(part), shares[i], sum_bufs, grad_half, span)
        for i, span in enumerate(SPANS)
    ]
    for one in sums:
        advance(one)
    advance(sharing)
    advance(sharing)
    advance(out_sum)
    loads[1].wait()
    for i in range(RING):
        left_side = normed_one[:, :, i * wide : (i + 1) * wide].reshape(wide, wide)
        grad_qkv[i] = dot(left_side, slices, (0, 0)).astype(LOW).reshape(RING, BLOCK, 384)
        if i % 2:
            advance(sums[i // 2])
    qkv_sum = plane_reduce_steps(mover, plane, grad_qkv, qkv_bufs[:5], qkv_bufs[5])
    advance(qkv_sum)
    advance(out_sum)
    gateup_swap = exchange_steps(mover, gateup_rows, gateup_got)
    advance(gateup_swap)
    down_swap = exchange_steps(mover, down_rows, down_got)
    advance(down_swap)
    gateup_got[z] = gateup_rows[z]
    down_got[z] = down_rows[z]
    advance(qkv_sum)
    advance(out_sum)
    advance(out_sum)
    spread_rows(out_bufs[5], out_send)
    out_swap = exchange_steps(mover, out_send, out_got)
    advance(out_swap)
    out_got[z] = out_send[z]
    advance(qkv_sum)
    for one in sums:
        advance(one)
    rows = tokens[half, :]
    inverse = lax.rsqrt(jnp.mean(rows * rows, axis=-1, keepdims=True) + eps_norm)
    unit = rows * inverse
    scaled = grad_half[...] * gain_ref[0:1, :]
    grad_tokens[half, :] = grad_rows[...] + inverse * (
        scaled - unit * jnp.mean(scaled * unit, axis=-1, keepdims=True)
    )
    share = mover.copy(grad_tokens.at[half], grad_tokens.at[half], sibling())
    advance(qkv_sum)
    advance(qkv_sum)
    spread_rows(qkv_bufs[5], qkv_send)
    qkv_swap = exchange_steps(mover, qkv_send, qkv_got)
    advance(qkv_swap)
    qkv_got[z] = qkv_send[z]
    width = gateup_got.shape[2]

    def with_weight(weight, got):
        return sum(
            jnp.sum(weight(j).astype(F32) * got[j].astype(F32), axis=-1, keepdims=True)
            for j in range(RING)
        )

    advance(gateup_swap)
    second = with_weight(lambda j: feed_rows[j, :, :width], gateup_got)
    advance(qkv_swap)
    kv_share = mover.copy(qkv_got.at[:, :, pl.ds(HD, 128)], kv_other, sibling())
    first = with_weight(lambda j: attn_rows[j, :, :384], qkv_got)
    scale_own[...] = jnp.where(lanes((PAD, 128)) == 0, first, second)
    scale_share = mover.copy(scale_own, scale_other, sibling())
    advance(down_swap)
    advance(out_swap)
    share.wait_recv()
    scale_share.wait_recv()
    scale_sums[...] = scale_own[...] + scale_other[...]
    kv_share.wait_recv()
    mover.finish()


def adam_kernel(
    rates,
    gateup_got,
    down_got,
    out_got,
    qkv_got,
    kv_other,
    output_in,
    tokens_in,
    *refs,
):
    core = lax.axis_index("tensor")
    inputs, results = refs[:15], refs[15:30]
    passed = refs[30:32]
    in_bufs, out_bufs = refs[32:47], refs[47:62]
    pass_bufs, in_sem, out_sem = refs[62:64], refs[64], refs[65]
    loads = [
        pltpu.make_async_copy(src, dst, in_sem.at[i])
        for i, (src, dst) in enumerate(
            zip((*inputs, output_in, tokens_in), (*in_bufs, *pass_bufs), strict=True)
        )
    ]
    stores = [
        pltpu.make_async_copy(src, dst, out_sem.at[i])
        for i, (src, dst) in enumerate(
            zip((*out_bufs, *pass_bufs), (*results, *passed), strict=True)
        )
    ]
    order = (3, 4, 0, 2, 1)
    for i in order:
        for one in loads[3 * i : 3 * i + 3]:
            one.start()
    for one in loads[15:]:
        one.start()
    low_lanes = lanes((OWN, 128)) < TAIL
    old = [in_bufs[3 * i : 3 * i + 3] for i in range(5)]
    new = [out_bufs[3 * i : 3 * i + 3] for i in range(5)]

    def rows(got, j, lo, n):
        return got[j, :, lo : lo + n].astype(F32)[:OWN]

    def join(one, two, offset):
        if offset:
            return jnp.where(low_lanes, pltpu.roll(one, TAIL, 1), two)
        return jnp.where(low_lanes, one, pltpu.roll(two, TAIL, 1))

    def tails(got, k, lo, offset=0):
        return join(rows(got, 2 * k, lo, 128), rows(got, 2 * k + 1, lo, 128), offset)

    def update(i, index, gradient):
        results = adam_update(*(ref[index] for ref in old[i][:1]), gradient, *(ref[index] for ref in old[i][1:]), rates[i], weight_decay)
        for ref, value in zip(new[i], results, strict=True):
            ref[index] = value

    every = slice(None)

    def ready(i):
        for one in loads[3 * i : 3 * i + 3]:
            one.wait()

    def done(i):
        for one in stores[3 * i : 3 * i + 3]:
            one.start()

    def main_place(j, width):
        return slice(width * j, width * (j + 1))

    def tail_place(k, width):
        return slice(RING * width + 128 * k, RING * width + 128 * (k + 1))

    ready(3)
    for g in range(2):
        for j in range(RING):
            update(3, (every, g, main_place(j, MAIN)), rows(gateup_got, j, MAIN * g, MAIN))
        for k in range(2):
            update(3, (every, g, tail_place(k, MAIN)), tails(gateup_got, k, 2 * MAIN, g))
    done(3)
    for one, two in zip(loads[15:], stores[15:], strict=True):
        one.wait()
        two.start()
    for i, got, width, main, tail in (
        (4, down_got, MAIN, 0, MAIN),
        (0, qkv_got, HD, 0, HD),
        (2, out_got, HD, 128, 0),
    ):
        ready(i)
        for j in range(RING):
            update(i, (every, main_place(j, width)), rows(got, j, main, width))
        for k in range(2):
            update(i, (every, tail_place(k, width)), tails(got, k, tail))
        done(i)
    ready(1)
    for k in range(2):
        place = slice(128 * k, 128 * (k + 1))
        own, theirs = tails(qkv_got, k, HD, 1), tails(kv_other, k, 0, 1)
        update(1, (every, 0, place), jnp.where(core == 0, own, theirs))
        update(1, (every, 1, place), jnp.where(core == 0, theirs, own))
    done(1)
    for one in stores:
        one.wait()


def run_adam(rates, grads, matrices, passing):
    flat = [array for triple in matrices for array in triple]
    shapes = [jax.ShapeDtypeStruct(array.shape, F32) for array in (*flat, *passing)]
    buffers = [pltpu.VMEM(array.shape, F32) for array in flat]
    results = pl.pallas_call(
        functools.partial(adam_kernel, rates),
        out_shape=shapes,
        in_specs=[pl.BlockSpec(memory_space=pltpu.VMEM)] * len(grads)
        + [pl.BlockSpec(memory_space=pl.ANY)] * len(shapes),
        out_specs=[pl.BlockSpec(memory_space=pl.ANY)] * len(shapes),
        scratch_shapes=[
            *buffers,
            *buffers,
            *(pltpu.VMEM(array.shape, F32) for array in passing),
            pltpu.SemaphoreType.DMA((len(shapes),)),
            pltpu.SemaphoreType.DMA((len(shapes),)),
        ],
        compiler_params=pltpu.CompilerParams(vmem_limit_bytes=60 * 1024 * 1024),
    )(*grads, *passing, *flat)
    return [results[3 * i : 3 * i + 3] for i in range(5)], results[15:]


def call(kernel, ident, copies, out, scratch, operands, spaces, out_spaces=None):
    results = pl.pallas_call(
        kernel,
        out_shape=[jax.ShapeDtypeStruct(shape, kind) for shape, kind in out.values()],
        in_specs=[pl.BlockSpec(memory_space=space) for space in spaces],
        out_specs=[pl.BlockSpec(memory_space=(out_spaces or {}).get(name, pltpu.VMEM)) for name in out],
        scratch_shapes=[
            pltpu.SemaphoreType.DMA((copies,)),
            pltpu.SemaphoreType.DMA((copies,)),
            pltpu.SemaphoreType.DMA((16,)),
            *scratch,
        ],
        compiler_params=pltpu.CompilerParams(
            collective_id=ident, has_side_effects=True, vmem_limit_bytes=60 * 1024 * 1024
        ),
    )(*operands)
    return dict(zip(out, results, strict=True))


def run_second(*operands):
    out = {
        "grad_rows": ((HALF, D), F32),
        "da_all": ((RING, BLOCK, D), LOW),
        "feed_part": ((RING, BLOCK, D), LOW),
        "gateup_grads": ((RING, RING, BLOCK, 2 * (MAIN + TAIL)), LOW),
        "down_rows": ((RING, PAD, 1024), LOW),
    }
    scratch = [
        pltpu.VMEM((RING, BLOCK, D), LOW),
        pltpu.VMEM((RING, BLOCK, D), LOW),
        pltpu.VMEM((RING, RING, BLOCK, 2 * (MAIN + TAIL)), LOW),
        pltpu.VMEM((RING, RING, BLOCK, 1024), LOW),
        pltpu.VMEM((RING * BLOCK, 1024), LOW),
        pltpu.VMEM((RING * BLOCK, 2 * (MAIN + TAIL)), LOW),
        pltpu.VMEM((RING, BLOCK, D), LOW),
        pltpu.VMEM((RING, BLOCK, 2 * (MAIN + TAIL)), LOW),
        pltpu.VMEM((HALF, D), F32),
        pltpu.VMEM((HALF, D), F32),
        pltpu.VMEM((HALF, D), F32),
        pltpu.VMEM((BLOCK, D), LOW),
        *reduce_scratch(),
        *plane_reduce_scratch(1024),
    ]
    spaces = [pl.ANY] * 5 + [pltpu.VMEM]
    return call(
        second_kernel, 5, 80, out, scratch, operands, spaces, {"gateup_grads": pl.ANY, "da_all": pl.ANY}
    )


def run_third(*operands):
    out = {
        "grad_out": ((RING, RING, BLOCK, 384), LOW),
        "grad_got": ((RING, BLOCK, 384), LOW),
        "gateup_rows": ((RING, PAD, 2 * (MAIN + TAIL)), LOW),
        "output": ((BLOCK, D), F32),
    }
    scratch = [
        pltpu.VMEM((RING, BLOCK, D), LOW),
        pltpu.VMEM((RING, RING, BLOCK, 128), LOW),
        pltpu.VMEM((RING, RING, BLOCK, HD), LOW),
        pltpu.VMEM((2, RING, RING, BLOCK, HD), LOW),
        pltpu.VMEM((RING, HALF, D), LOW),
        pltpu.VMEM((HALF, D), F32),
        pltpu.VMEM((RING, BLOCK, 384), LOW),
        pltpu.VMEM((RING, BLOCK, 384), LOW),
        pltpu.VMEM((5, BLOCK, HD), LOW),
        pltpu.VMEM((5, BLOCK, 128), F32),
        pltpu.VMEM((5, BLOCK, RING * BLOCK), LOW),
        pltpu.VMEM((5, BLOCK, RING * BLOCK), LOW),
        pltpu.VMEM((5, BLOCK, HD), F32),
        pltpu.VMEM((2, RING, RING, BLOCK, HD), LOW),
        pltpu.VMEM((RING, RING, BLOCK, HD), LOW),
        pltpu.VMEM((RING, RING, BLOCK, HD), LOW),
        pltpu.VMEM((5, BLOCK, HD), F32),
        pltpu.VMEM((RING, BLOCK, 384), LOW),
        pltpu.VMEM((BLOCK, HD), F32),
        *reduce_scratch(),
        *plane_reduce_scratch(2 * (MAIN + TAIL)),
        *plane_reduce_scratch(HD),
    ]
    spaces = [pl.ANY] * 3 + [pltpu.VMEM] + [pl.ANY] * 2 + [pltpu.VMEM] * 2 + [pl.ANY] + [pltpu.VMEM] * 6
    return call(third_kernel, 2, 100, out, scratch, operands, spaces)


def run_fourth(*operands):
    out = {
        "grad_tokens": ((BLOCK, D), F32),
        "gateup_got": ((RING, PAD, 2 * (MAIN + TAIL)), LOW),
        "down_got": ((RING, PAD, 1024), LOW),
        "out_got": ((RING, PAD, 384), LOW),
        "qkv_got": ((RING, PAD, 384), LOW),
        "kv_other": ((RING, PAD, 128), LOW),
        "scale_sums": ((PAD, 128), F32),
    }
    scratch = [
        pltpu.VMEM((RING, RING, BLOCK, 384), LOW),
        pltpu.VMEM((RING, BLOCK, D), LOW),
        pltpu.VMEM((RING, BLOCK, D), LOW),
        pltpu.VMEM((HALF, D), F32),
        pltpu.VMEM((RING, RING, BLOCK, 384), LOW),
        pltpu.VMEM((RING, PAD, 384), LOW),
        pltpu.VMEM((RING, PAD, 384), LOW),
        pltpu.VMEM((PAD, 128), F32),
        pltpu.VMEM((PAD, 128), F32),
        *reduce_scratch(),
        *plane_reduce_scratch(384),
        *plane_reduce_scratch(384),
    ]
    spaces = [pltpu.VMEM] * 4 + [pl.ANY] * 2 + [pltpu.VMEM] * 5
    return call(fourth_kernel, 3, 80, out, scratch, operands, spaces)


def adam_update(weight, gradient, first_moment, second_moment, learn_rate, decay_rate):
    first_moment = first_decay * first_moment + (1.0 - first_decay) * gradient
    second_moment = second_decay * second_moment + (1.0 - second_decay) * gradient * gradient
    corrected = (
        first_moment
        / (1.0 - first_decay**STEP)
        / (jnp.sqrt(second_moment / (1.0 - second_decay**STEP)) + adam_eps)
    )
    return (weight - learn_rate * (corrected + decay_rate * weight), first_moment, second_moment)


def out_fan_in(seq_length):
    return max(1, H * HD * 4 // min(WINDOW, seq_length))


def per_device(
    tokens,
    cotangent,
    w_query,
    w_keyvalue,
    w_out,
    w_gateup,
    w_down,
    norm_scales,
    first_query,
    first_keyvalue,
    first_out,
    first_gateup,
    first_down,
    first_scales,
    second_query,
    second_keyvalue,
    second_out,
    second_gateup,
    second_down,
    second_scales,
):
    core = lax.axis_index("tensor")
    seq_index = lax.axis_index("x") * RING + lax.axis_index("z")
    positions = seq_index * BLOCK + jnp.arange(BLOCK, dtype=jnp.int32)
    seq_length = BLOCK * RING * RING

    frequency = 10000.0 ** (-jnp.arange(TAIL, dtype=F32) / TAIL)
    angles = positions.astype(F32)[:, None] * frequency[None, :]
    cos_table = jnp.tile(jnp.cos(angles), (1, 2))
    sin_table = jnp.concatenate([-jnp.sin(angles), jnp.sin(angles)], axis=1)
    cos_kv = jnp.where(core == 0, cos_table, 1.0)
    sin_kv = jnp.where(core == 0, sin_table, 0.0)
    first = run_first(
        w_query,
        w_keyvalue,
        w_out.T,
        w_gateup,
        w_down.T,
        jnp.pad(norm_scales.T, ((0, 0), (TAIL, 128 - TAIL - 2))),
        tokens,
        cotangent,
        cos_table,
        sin_table,
        cos_kv,
        sin_kv,
    )
    second = run_second(
        first["feed_full"],
        first["normed_two"],
        first["dy_all"],
        cotangent,
        first["residual"],
        first["gains"],
    )
    third = run_third(
        second["feed_part"],
        second["gateup_grads"],
        second["da_all"],
        first["residual"],
        first["attn_a"],
        first["attn_b"],
        first["att_slice"],
        first["query"],
        first["keyvalue"],
        first["log_total"],
        first["attended"],
        cos_table,
        sin_table,
        cos_kv,
        sin_kv,
    )
    fourth = run_fourth(
        third["grad_got"],
        third["gateup_rows"],
        second["down_rows"],
        third["grad_out"],
        first["attn_a"],
        first["normed_one"],
        second["grad_rows"],
        tokens,
        first["gains"],
        first["attn_rows"],
        first["feed_rows"],
    )
    matrix_rate = 2.0 * D ** (-0.5)
    out_rate = 2.0 * out_fan_in(seq_length) ** (-0.5)
    down_rate = 2.0 * (FF // 2) ** (-0.5)
    triples, (output, grad_tokens) = run_adam(
        (matrix_rate, matrix_rate, out_rate, matrix_rate, down_rate),
        [fourth[name] for name in ("gateup_got", "down_got", "out_got", "qkv_got", "kv_other")],
        [
            (w_query, first_query, second_query),
            (w_keyvalue, first_keyvalue, second_keyvalue),
            (w_out.T, first_out.T, second_out.T),
            (w_gateup, first_gateup, second_gateup),
            (w_down.T, first_down.T, second_down.T),
        ],
        (third["output"], fourth["grad_tokens"]),
    )
    triples[2] = [array.T for array in triples[2]]
    triples[4] = [array.T for array in triples[4]]
    scale_grads = fourth["scale_sums"][:OWN, :2].T / (1.0 + norm_scales.astype(LOW).astype(F32))
    triples.append(
        adam_update(norm_scales, scale_grads, first_scales, second_scales, gain_rate, 0.0)
    )
    return (output, grad_tokens, *(triple[i] for i in range(3) for triple in triples))


def solution(mesh):
    split = Mesh(
        mesh.devices.reshape(RING, RING, RING, 2), ("dp", "x", "z", "tensor")
    )
    rows = ("dp", "x", "z")
    matrices = (
        P(rows, "tensor"),
        P(rows, None, None),
        P("tensor", rows),
        P(rows, None, "tensor"),
        P("tensor", rows),
        P(None, rows),
    )
    in_specs = (P(rows, None), P(rows, None), *matrices, *matrices, *matrices)
    out_specs = in_specs
    return jax.shard_map(
        per_device, mesh=split, in_specs=in_specs, out_specs=out_specs, check_vma=False
    )
```

profile of v0, /device:TPU:1, one launch (start us, length us, event | category | flops | bytes accessed | tf_op | source)
XLA Modules:
  0.0 371.4 jit_solution(12477115413487856059)
XLA Ops:
  0.7 0.4 fusion
  1.1 0.1 copy.78
  1.2 0.1 copy.80.cos_ref
  1.3 0.0 copy-start
  1.3 0.8 broadcast_select_fusion
  2.1 0.8 copy.76
  2.9 0.7 pad.4.scale_columns
  3.6 146.3 %shard_map.347 = (bf16[4,4,160,2944]{3,2,1,0:T(8,128)(2,1)}, bf16[4,4,160,512]{3,2,1,0:T(8,128)(2,1)}, bf16[4,4,160,256]{3,2,1,0:T(8,128)(2,1)}, bf16[4,160,2560...) custom-call(f32[40,1280]{1,0:T(8,128)} %refs_0_.1, ...), custom_call_target="tpu_custom_call" | custom-call | tf_op jit(solution)/shard_map/pallas_call | solution.py:1377
  149.9 79.0 %shard_map.348 = (f32[80,2560]{1,0:T(8,128)}, bf16[4,160,2560]{2,1,0:T(8,128)(2,1)}, bf16[4,160,2560]{2,1,0:T(8,128)(2,1)}, bf16[4,4,160,1920]{3,2,1,0:T(8,128)(2,1)}, bf16[4,48,1024]{2,1,0:T(8,128)(2,1)}) custom-call(bf16[4,4,160,2944]{3,2,1,0:T(8,128)(2,1)} %get-tuple-element.68.feed_full, bf16[4,160,2560]{2,1,0:T(8,128)(2,1)} %get-tuple-element.69.normed_two, ...), custom_call_target="tpu_custom_call" | custom-call | tf_op jit(solution)/shard_map/pallas_call | solution.py:1377
  228.9 77.0 %shard_map.349 = (bf16[4,4,160,384]{3,2,1,0:T(8,128)(2,1)}, bf16[4,160,384]{2,1,0:T(8,128)(2,1)}, bf16[4,48,1920]{2,1,0:T(8,128)(2,1)}, f32[160,2560]{1,0:T(8,128)}) custom-call(bf16[4,160,2560]{2,1,0:T(8,128)(2,1)} %get-tuple-element.73.feed_part, bf16[4,4,160,1920]{3,2,1,0:T(8,128)(2,1)} %get-tuple-element.74.gateup_grads, ...), custom_call_target="tpu_custom_call" | custom-call | tf_op jit(solution)/shard_map/pallas_call | solution.py:1377
  305.9 0.0 copy-start.1
  305.9 0.0 copy-start.3
  305.9 50.3 %shard_map.350 = (f32[160,2560]{1,0:T(8,128)}, bf16[4,48,1920]{2,1,0:T(8,128)(2,1)}, bf16[4,48,1024]{2,1,0:T(8,128)(2,1)}, bf16[4,48,384]{2,1,0:T(8,128)(2,1)}, ...) custom-call(bf16[4,160,384]{2,1,0:T(8,128)(2,1)} %get-tuple-element.83.grad_got, ...), custom_call_target="tpu_custom_call" | custom-call | tf_op jit(solution)/shard_map/pallas_call | solution.py:1377
  356.2 0.1 copy.82
  356.3 0.1 copy.83
  356.4 0.1 copy.84
  356.5 0.8 sqrt_add_fusion
  357.3 0.1 copy.85
  357.3 0.1 copy.86
  357.4 0.1 copy.88
  357.5 0.6 copy.89
  358.2 11.5 %shard_map.351 = (f32[40,1280]{1,0:T(8,128)}, f32[40,1280]{1,0:T(8,128)}, f32[40,1280]{1,0:T(8,128)}, f32[40,2,256]{2,1,0:T(2,128)}, f32[40,2,256]{2,1,0:T(2,128...) custom-call(bf16[4,48,1920]{2,1,0:T(8,128)(2,1)} %get-tuple-element., ...), custom_call_target="tpu_custom_call" | custom-call | tf_op jit(solution)/shard_map/pallas_call | solution.py:1358
  369.7 0.6 copy.90
  370.3 0.6 copy.91
  (13 shorter events, 0.1 us)
Async XLA Ops:
  1.3 2.3 copy-start
  305.9 50.3 %copy-start.1 = (f32[2,40]{1,0:T(2,128)S(1)}, f32[2,40]{1,0:T(2,128)}, u32[]{:S(2)}) copy-start(f32[2,40]{1,0:T(2,128)} %param.27) | copy-start | bytes 964
  305.9 50.4 %copy-start.2 = (f32[2,40]{1,0:T(2,128)S(1)}, f32[2,40]{1,0:T(2,128)}, u32[]{:S(2)}) copy-start(f32[2,40]{1,0:T(2,128)} %param.33) | copy-start | bytes 964
  305.9 50.5 %copy-start.3 = (f32[2,40]{1,0:T(2,128)S(1)}, f32[2,40]{1,0:T(2,128)}, u32[]{:S(2)}) copy-start(f32[2,40]{1,0:T(2,128)} %param.39) | copy-start | bytes 964
where the time goes:
time: 377 us; the launch traced here: 371 us
  Pallas kernels  364 us (97%)
  local copies, waits for them, and re-layouts  4.08 us (1%)
    pallas_call x4, Pallas kernels, call(): pl.pallas_call(kernel, out_shape=[jax.ShapeDtypeStruct(shape, kind) for s...  353 us
    pallas_call x1, Pallas kernels, run_adam(): pl.pallas_call(functools.partial(adam_kernel, rates), out_shape=shapes, i...  11.5 us

commit v1 on v0

--- a/solution.py
+++ b/solution.py
@@ -1090,6 +1090,7 @@
         grad_send[h, :, :HD] = grad_query[h].astype(LOW)
     advance(kv_sum)
     advance(kv_sum)
+    advance(rows_sum)
     advance(kv_sum)
     advance(kv_sum)
     kv_low[:, :128] = turn(kv_rows[:, :128], cos_kv[...], -sin_kv[...])
@@ -1105,12 +1106,11 @@
     swap = exchange_steps(mover, grad_send, grad_got)
     advance(swap)
     grad_got[z] = grad_send[z]
+    advance(rows_sum)
     advance(feed_sum)
     output[half, :] = residual[half, :] + out_half[...]
     out_share = mover.copy(output.at[half], output.at[half], sibling())
-    advance(rows_sum)
     advance(swap)
-    advance(rows_sum)
     advance(rows_sum)
     spread_rows(rows_res, gateup_rows)
     out_share.wait_recv()
@@ -1163,10 +1163,16 @@
         load.start()
     greet([{"z": step("z", d)} for d in (1, 2, 3)] + plane_peers(plane) + [sibling()])
     mover = Mover(send_sem, recv_sem)
+    slices = grad_got[...].reshape(RING * BLOCK, 384)
+    wide = RING * BLOCK
+    loads[1].wait()
+    for i in range(RING):
+        left_side = normed_one[:, :, i * wide : (i + 1) * wide].reshape(wide, wide)
+        grad_qkv[i] = dot(left_side, slices, (0, 0)).astype(LOW).reshape(RING, BLOCK, 384)
+    qkv_sum = plane_reduce_steps(mover, plane, grad_qkv, qkv_bufs[:5], qkv_bufs[5])
+    advance(qkv_sum)
     out_sum = plane_reduce_steps(mover, plane, grad_out, out_bufs[:5], out_bufs[5])
     advance(out_sum)
-    slices = grad_got[...].reshape(RING * BLOCK, 384)
-    wide = RING * BLOCK
     loads[0].wait()
     weight = qkv_weight[...].reshape(D, 384)
 
@@ -1185,29 +1191,18 @@
         advance(one)
     advance(sharing)
     advance(sharing)
+    advance(qkv_sum)
+    for one in sums:
+        advance(one)
     advance(out_sum)
-    loads[1].wait()
-    for i in range(RING):
-        left_side = normed_one[:, :, i * wide : (i + 1) * wide].reshape(wide, wide)
-        grad_qkv[i] = dot(left_side, slices, (0, 0)).astype(LOW).reshape(RING, BLOCK, 384)
-        if i % 2:
-            advance(sums[i // 2])
-    qkv_sum = plane_reduce_steps(mover, plane, grad_qkv, qkv_bufs[:5], qkv_bufs[5])
     advance(qkv_sum)
-    advance(out_sum)
     gateup_swap = exchange_steps(mover, gateup_rows, gateup_got)
     advance(gateup_swap)
     down_swap = exchange_steps(mover, down_rows, down_got)
     advance(down_swap)
     gateup_got[z] = gateup_rows[z]
     down_got[z] = down_rows[z]
-    advance(qkv_sum)
     advance(out_sum)
-    advance(out_sum)
-    spread_rows(out_bufs[5], out_send)
-    out_swap = exchange_steps(mover, out_send, out_got)
-    advance(out_swap)
-    out_got[z] = out_send[z]
     advance(qkv_sum)
     for one in sums:
         advance(one)
@@ -1219,12 +1214,17 @@
         scaled - unit * jnp.mean(scaled * unit, axis=-1, keepdims=True)
     )
     share = mover.copy(grad_tokens.at[half], grad_tokens.at[half], sibling())
-    advance(qkv_sum)
+    advance(out_sum)
     advance(qkv_sum)
     spread_rows(qkv_bufs[5], qkv_send)
     qkv_swap = exchange_steps(mover, qkv_send, qkv_got)
     advance(qkv_swap)
     qkv_got[z] = qkv_send[z]
+    advance(out_sum)
+    spread_rows(out_bufs[5], out_send)
+    out_swap = exchange_steps(mover, out_send, out_got)
+    advance(out_swap)
+    out_got[z] = out_send[z]
     width = gateup_got.shape[2]
 
     def with_weight(weight, got):

time: 377 us -> 371 us (0.984)
  Pallas kernels: 364 us -> 359 us
    pallas_call x4, Pallas kernels: 353 us -> 347 us  [call(): pl.pallas_call(kernel, out_shape=[jax.ShapeDtypeStruct(shape, kind) for s...]
where the time goes in v1:
time: 371 us; the launch traced here: 366 us
  Pallas kernels  359 us (97%)
  local copies, waits for them, and re-layouts  4.08 us (1%)
    pallas_call x4, Pallas kernels, call(): pl.pallas_call(kernel, out_shape=[jax.ShapeDtypeStruct(shape, kind) for s...  347 us
    pallas_call x1, Pallas kernels, run_adam(): pl.pallas_call(functools.partial(adam_kernel, rates), out_shape=shapes, i...  11.5 us

profile of v1, /device:TPU:1, one launch (start us, length us, event | category | flops | bytes accessed | tf_op | source)
XLA Modules:
  0.0 365.9 jit_solution(15147142369851449146)
XLA Ops:
  0.7 0.4 fusion
  1.1 0.1 copy.78
  1.2 0.1 copy.80.cos_ref
  1.3 0.0 copy-start
  1.3 0.8 broadcast_select_fusion
  2.1 0.8 copy.76
  2.9 0.7 pad.4.scale_columns
  3.6 146.3 %shard_map.347 = (bf16[4,4,160,2944]{3,2,1,0:T(8,128)(2,1)}, bf16[4,4,160,512]{3,2,1,0:T(8,128)(2,1)}, bf16[4,4,160,256]{3,2,1,0:T(8,128)(2,1)}, bf16[4,160,2560...) custom-call(f32[40,1280]{1,0:T(8,128)} %refs_0_.1, ...), custom_call_target="tpu_custom_call" | custom-call | tf_op jit(solution)/shard_map/pallas_call | solution.py:1377
  149.9 79.0 %shard_map.348 = (f32[80,2560]{1,0:T(8,128)}, bf16[4,160,2560]{2,1,0:T(8,128)(2,1)}, bf16[4,160,2560]{2,1,0:T(8,128)(2,1)}, bf16[4,4,160,1920]{3,2,1,0:T(8,128)(2,1)}, bf16[4,48,1024]{2,1,0:T(8,128)(2,1)}) custom-call(bf16[4,4,160,2944]{3,2,1,0:T(8,128)(2,1)} %get-tuple-element.68.feed_full, bf16[4,160,2560]{2,1,0:T(8,128)(2,1)} %get-tuple-element.69.normed_two, ...), custom_call_target="tpu_custom_call" | custom-call | tf_op jit(solution)/shard_map/pallas_call | solution.py:1377
  228.9 72.2 %shard_map.349 = (bf16[4,4,160,384]{3,2,1,0:T(8,128)(2,1)}, bf16[4,160,384]{2,1,0:T(8,128)(2,1)}, bf16[4,48,1920]{2,1,0:T(8,128)(2,1)}, f32[160,2560]{1,0:T(8,128)}) custom-call(bf16[4,160,2560]{2,1,0:T(8,128)(2,1)} %get-tuple-element.73.feed_part, bf16[4,4,160,1920]{3,2,1,0:T(8,128)(2,1)} %get-tuple-element.74.gateup_grads, ...), custom_call_target="tpu_custom_call" | custom-call | tf_op jit(solution)/shard_map/pallas_call | solution.py:1377
  301.1 0.0 copy-start.1
  301.1 0.0 copy-start.3
  301.1 49.7 %shard_map.350 = (f32[160,2560]{1,0:T(8,128)}, bf16[4,48,1920]{2,1,0:T(8,128)(2,1)}, bf16[4,48,1024]{2,1,0:T(8,128)(2,1)}, bf16[4,48,384]{2,1,0:T(8,128)(2,1)}, ...) custom-call(bf16[4,160,384]{2,1,0:T(8,128)(2,1)} %get-tuple-element.83.grad_got, ...), custom_call_target="tpu_custom_call" | custom-call | tf_op jit(solution)/shard_map/pallas_call | solution.py:1377
  350.8 0.1 copy.82
  350.9 0.1 copy.83
  351.0 0.1 copy.84
  351.1 0.8 sqrt_add_fusion
  351.8 0.1 copy.85
  351.9 0.1 copy.86
  352.0 0.1 copy.88
  352.1 0.6 copy.89
  352.7 11.5 %shard_map.351 = (f32[40,1280]{1,0:T(8,128)}, f32[40,1280]{1,0:T(8,128)}, f32[40,1280]{1,0:T(8,128)}, f32[40,2,256]{2,1,0:T(2,128)}, f32[40,2,256]{2,1,0:T(2,128...) custom-call(bf16[4,48,1920]{2,1,0:T(8,128)(2,1)} %get-tuple-element., ...), custom_call_target="tpu_custom_call" | custom-call | tf_op jit(solution)/shard_map/pallas_call | solution.py:1358
  364.2 0.6 copy.90
  364.9 0.6 copy.91
  (13 shorter events, 0.1 us)
Async XLA Ops:
  1.3 2.3 copy-start
  301.1 49.7 %copy-start.1 = (f32[2,40]{1,0:T(2,128)S(1)}, f32[2,40]{1,0:T(2,128)}, u32[]{:S(2)}) copy-start(f32[2,40]{1,0:T(2,128)} %param.27) | copy-start | bytes 964
  301.1 49.8 %copy-start.2 = (f32[2,40]{1,0:T(2,128)S(1)}, f32[2,40]{1,0:T(2,128)}, u32[]{:S(2)}) copy-start(f32[2,40]{1,0:T(2,128)} %param.33) | copy-start | bytes 964
  301.1 49.9 %copy-start.3 = (f32[2,40]{1,0:T(2,128)S(1)}, f32[2,40]{1,0:T(2,128)}, u32[]{:S(2)}) copy-start(f32[2,40]{1,0:T(2,128)} %param.39) | copy-start | bytes 964

commit v2 on v1

--- a/solution.py
+++ b/solution.py
@@ -496,6 +496,7 @@
         gathers.append(gather_steps(mover, normed_low, normed_two, span))
         advance(gathers[-1])
         res_shares.append(mover.copy(residual.at[place], residual.at[place], sibling()))
+        advance(feed_gather)
     advance(dy_gather)
     for copy in res_shares:
         copy.wait_recv()
@@ -504,8 +505,6 @@
     save(normed_low, normed_two.at[z])
     for one in gathers:
         advance(one)
-    advance(feed_gather)
-    advance(feed_gather)
     for one in gathers:
         advance(one)
     advance(dy_gather)

time: 371 us -> 362 us (0.976)
  Pallas kernels: 359 us -> 350 us
    pallas_call x4, Pallas kernels: 347 us -> 338 us  [call(): pl.pallas_call(kernel, out_shape=[jax.ShapeDtypeStruct(shape, kind) for s...]
where the time goes in v2:
time: 362 us; the launch traced here: 357 us
  Pallas kernels  350 us (97%)
  local copies, waits for them, and re-layouts  4.08 us (1%)
    pallas_call x4, Pallas kernels, call(): pl.pallas_call(kernel, out_shape=[jax.ShapeDtypeStruct(shape, kind) for s...  338 us
    pallas_call x1, Pallas kernels, run_adam(): pl.pallas_call(functools.partial(adam_kernel, rates), out_shape=shapes, i...  11.5 us

profile of v2, /device:TPU:1, one launch (start us, length us, event | category | flops | bytes accessed | tf_op | source)
XLA Modules:
  0.0 356.9 jit_solution(1466141886746552939)
XLA Ops:
  0.7 0.4 fusion
  1.1 0.1 copy.78
  1.2 0.1 copy.80.cos_ref
  1.3 0.0 copy-start
  1.3 0.8 broadcast_select_fusion
  2.1 0.8 copy.76
  2.9 0.7 pad.4.scale_columns
  3.6 140.3 %shard_map.347 = (bf16[4,4,160,2944]{3,2,1,0:T(8,128)(2,1)}, bf16[4,4,160,512]{3,2,1,0:T(8,128)(2,1)}, bf16[4,4,160,256]{3,2,1,0:T(8,128)(2,1)}, bf16[4,160,2560...) custom-call(f32[40,1280]{1,0:T(8,128)} %refs_0_.1, ...), custom_call_target="tpu_custom_call" | custom-call | tf_op jit(solution)/shard_map/pallas_call | solution.py:1376
  143.9 77.0 %shard_map.348 = (f32[80,2560]{1,0:T(8,128)}, bf16[4,160,2560]{2,1,0:T(8,128)(2,1)}, bf16[4,160,2560]{2,1,0:T(8,128)(2,1)}, bf16[4,4,160,1920]{3,2,1,0:T(8,128)(2,1)}, bf16[4,48,1024]{2,1,0:T(8,128)(2,1)}) custom-call(bf16[4,4,160,2944]{3,2,1,0:T(8,128)(2,1)} %get-tuple-element.68.feed_full, bf16[4,160,2560]{2,1,0:T(8,128)(2,1)} %get-tuple-element.69.normed_two, ...), custom_call_target="tpu_custom_call" | custom-call | tf_op jit(solution)/shard_map/pallas_call | solution.py:1376
  220.9 69.2 %shard_map.349 = (bf16[4,4,160,384]{3,2,1,0:T(8,128)(2,1)}, bf16[4,160,384]{2,1,0:T(8,128)(2,1)}, bf16[4,48,1920]{2,1,0:T(8,128)(2,1)}, f32[160,2560]{1,0:T(8,128)}) custom-call(bf16[4,160,2560]{2,1,0:T(8,128)(2,1)} %get-tuple-element.73.feed_part, bf16[4,4,160,1920]{3,2,1,0:T(8,128)(2,1)} %get-tuple-element.74.gateup_grads, ...), custom_call_target="tpu_custom_call" | custom-call | tf_op jit(solution)/shard_map/pallas_call | solution.py:1376
  290.1 0.0 copy-start.1
  290.1 0.0 copy-start.2
  290.1 51.6 %shard_map.350 = (f32[160,2560]{1,0:T(8,128)}, bf16[4,48,1920]{2,1,0:T(8,128)(2,1)}, bf16[4,48,1024]{2,1,0:T(8,128)(2,1)}, bf16[4,48,384]{2,1,0:T(8,128)(2,1)}, ...) custom-call(bf16[4,160,384]{2,1,0:T(8,128)(2,1)} %get-tuple-element.83.grad_got, ...), custom_call_target="tpu_custom_call" | custom-call | tf_op jit(solution)/shard_map/pallas_call | solution.py:1376
  341.8 0.1 copy.82
  341.9 0.1 copy.83
  342.0 0.1 copy.84
  342.1 0.8 sqrt_add_fusion
  342.8 0.1 copy.85
  342.9 0.1 copy.86
  343.0 0.1 copy.88
  343.1 0.6 copy.89
  343.7 11.5 %shard_map.351 = (f32[40,1280]{1,0:T(8,128)}, f32[40,1280]{1,0:T(8,128)}, f32[40,1280]{1,0:T(8,128)}, f32[40,2,256]{2,1,0:T(2,128)}, f32[40,2,256]{2,1,0:T(2,128...) custom-call(bf16[4,48,1920]{2,1,0:T(8,128)(2,1)} %get-tuple-element., ...), custom_call_target="tpu_custom_call" | custom-call | tf_op jit(solution)/shard_map/pallas_call | solution.py:1357
  355.2 0.6 copy.90
  355.8 0.6 copy.91
  (13 shorter events, 0.1 us)
Async XLA Ops:
  1.3 2.3 copy-start
  290.1 51.6 %copy-start.1 = (f32[2,40]{1,0:T(2,128)S(1)}, f32[2,40]{1,0:T(2,128)}, u32[]{:S(2)}) copy-start(f32[2,40]{1,0:T(2,128)} %param.27) | copy-start | bytes 964
  290.1 51.7 %copy-start.2 = (f32[2,40]{1,0:T(2,128)S(1)}, f32[2,40]{1,0:T(2,128)}, u32[]{:S(2)}) copy-start(f32[2,40]{1,0:T(2,128)} %param.33) | copy-start | bytes 964
  290.1 51.8 %copy-start.3 = (f32[2,40]{1,0:T(2,128)S(1)}, f32[2,40]{1,0:T(2,128)}, u32[]{:S(2)}) copy-start(f32[2,40]{1,0:T(2,128)} %param.39) | copy-start | bytes 964
